TPU v7x, 512 devices: a whole 4x8x8 slice. The times are simulated.
512 devices in a mesh: src: 64 (over x, y_hi, z), tgt: 8 (over y_lo, core).
Axes of the slice: x: 4, y: 8 (y_hi: 2, y_lo: 4; y = y_hi * 4 + y_lo), z: 8, core: 2. Of those that a mesh axis runs over, the one named last changes fastest.
Arguments:
- source_points: float32 [32, 16384], P(None, 'src'), may hold values from -1.5 to 1.5
- source_potential: float32 [16384], P('src'), may hold values from 2 to 4
- source_cotangent: float32 [16384], P('src'), may hold values from -25 to 25
- target_points: float32 [32, 32768], P(None, 'tgt'), may hold values from -1.5 to 1.5
- target_potential: float32 [32768], P('tgt'), may hold values from 2 to 4
- target_cotangent: float32 [32768], P('tgt'), may hold values from -25 to 25
Outputs:
- source_adjoint: float32 [16384], P('src')
- target_adjoint: float32 [32768], P('tgt')
- source_gradient: float32 [32, 16384], P(None, 'src')
- target_gradient: float32 [32, 32768], P(None, 'tgt')
All inputs are finite; a program needn't handle non-finite values.
Results may differ from a plain program's by a relative error of at most 0.0003.
Values sent between devices are 32-bit elements; how exact they have to be, the bound alone decides.
A program may use at most 64 MiB of HBM per device.

v0:
```python
import math

import jax
import jax.numpy as jnp
from jax import lax
from jax.sharding import PartitionSpec as P

ITERS = 2


epsilon = 0.5
ridge = 0.5
highest = lax.Precision.HIGHEST


def transport_tile(
    source_points, source_norms, source_potential, target_block, target_potential_block, factor
):
    cross_terms = lax.dot_general(
        source_points,
        target_block,
        (((0,), (0,)), ((), ())),
        precision=highest,
        preferred_element_type=jnp.float32,
    )
    target_norms = jnp.sum(target_block * target_block, axis=0)
    distance = source_norms[:, None] + target_norms[None, :] - 2.0 * cross_terms
    return (
        jnp.exp(source_potential[:, None] + target_potential_block[None, :] - distance / epsilon)
        * factor
    )


def local(
    source_points,
    source_potential,
    source_cotangent,
    target_points,
    target_potential,
    target_cotangent,
):
    source_count = source_points.shape[1]
    target_count = target_points.shape[1]
    factor = 1.0 / math.sqrt(
        source_count * lax.axis_size("src") * target_count * lax.axis_size("tgt")
    )
    source_share = 1.0 / lax.axis_size("tgt")
    target_share = 1.0 / lax.axis_size("src")
    block_width = min(512, target_count)
    block_total = target_count // block_width
    source_norms = jnp.sum(source_points * source_points, axis=0)

    def tile_at(offset):
        target_block = lax.dynamic_slice_in_dim(target_points, offset, block_width, 1)
        potential_block = lax.dynamic_slice_in_dim(target_potential, offset, block_width, 0)
        return (
            target_block,
            transport_tile(
                source_points, source_norms, source_potential, target_block, potential_block, factor
            ),
        )

    def local_inner(first_source, second_source, first_target, second_target):
        return (
            jnp.sum(first_source * second_source) * source_share
            + jnp.sum(first_target * second_target) * target_share
        )

    def squared_norm(vector_source, vector_target):
        return lax.psum(
            local_inner(vector_source, vector_source, vector_target, vector_target), ("src", "tgt")
        )

    adjoint_source = jnp.zeros_like(source_cotangent)
    adjoint_target = jnp.zeros_like(target_cotangent)
    residual_source, residual_target = (source_cotangent, target_cotangent)
    direction_source, direction_target = (source_cotangent, target_cotangent)
    norm_now = squared_norm(residual_source, residual_target)
    margins = None
    for iteration in range(ITERS):
        operator_margins = margins
        if operator_margins is None:
            operator_source_vectors = jnp.stack([jnp.ones_like(direction_source), direction_source])
            operator_target_vectors = jnp.stack([jnp.ones_like(direction_target), direction_target])
        else:
            operator_source_vectors = direction_source[None, :]
            operator_target_vectors = direction_target[None, :]
        source_vectors = operator_source_vectors
        target_vectors = operator_target_vectors

        def advance(block_id, totals):
            row_total, column_total = totals
            offset = block_id * block_width
            target_block, transport = tile_at(offset)
            vector_block = lax.dynamic_slice_in_dim(target_vectors, offset, block_width, 1)
            row_total = row_total + lax.dot_general(
                vector_block,
                transport,
                (((1,), (1,)), ((), ())),
                precision=highest,
                preferred_element_type=jnp.float32,
            )
            column_part = jnp.dot(
                source_vectors, transport, precision=highest, preferred_element_type=jnp.float32
            )
            column_total = lax.dynamic_update_slice_in_dim(column_total, column_part, offset, 1)
            return (row_total, column_total)

        products_initial = (
            jnp.zeros((target_vectors.shape[0], source_count), jnp.float32),
            jnp.zeros((source_vectors.shape[0], target_count), jnp.float32),
        )
        operator_row_total, operator_column_total = lax.fori_loop(
            0, block_total, advance, products_initial
        )
        operator_row_total = lax.psum(operator_row_total, "tgt")
        operator_column_total = lax.psum(operator_column_total, "src")
        if operator_margins is None:
            operator_margins = (operator_row_total[0], operator_column_total[0])
        image_source = (operator_margins[0] + ridge) * direction_source + operator_row_total[-1]
        image_target = (operator_margins[1] + ridge) * direction_target + operator_column_total[-1]
        image_source, image_target, margins = (image_source, image_target, operator_margins)
        curve_value = lax.psum(
            local_inner(direction_source, image_source, direction_target, image_target),
            ("src", "tgt"),
        )
        step_size = norm_now / curve_value
        adjoint_source = adjoint_source + step_size * direction_source
        adjoint_target = adjoint_target + step_size * direction_target
        residual_source = residual_source - step_size * image_source
        residual_target = residual_target - step_size * image_target
        if iteration + 1 < ITERS:
            norm_next = squared_norm(residual_source, residual_target)
            direction_ratio = norm_next / norm_now
            direction_source = residual_source + direction_ratio * direction_source
            direction_target = residual_target + direction_ratio * direction_target
            norm_now = norm_next

    def gradient_step(block_id, totals):
        row_weight, row_points, column_weight, column_points = totals
        offset = block_id * block_width
        target_block, transport = tile_at(offset)
        adjoint_block = lax.dynamic_slice_in_dim(adjoint_target, offset, block_width, 0)
        weight = transport * (adjoint_source[:, None] + adjoint_block[None, :])
        row_weight = row_weight + jnp.sum(weight, axis=1)
        row_points = row_points + lax.dot_general(
            target_block,
            weight,
            (((1,), (1,)), ((), ())),
            precision=highest,
            preferred_element_type=jnp.float32,
        )
        column_weight = lax.dynamic_update_slice_in_dim(
            column_weight, jnp.sum(weight, axis=0), offset, 0
        )
        column_part = jnp.dot(
            source_points, weight, precision=highest, preferred_element_type=jnp.float32
        )
        column_points = lax.dynamic_update_slice_in_dim(column_points, column_part, offset, 1)
        return (row_weight, row_points, column_weight, column_points)

    initial = (
        jnp.zeros((source_count,), jnp.float32),
        jnp.zeros(source_points.shape, jnp.float32),
        jnp.zeros((target_count,), jnp.float32),
        jnp.zeros(target_points.shape, jnp.float32),
    )
    row_weight, row_points, column_weight, column_points = lax.fori_loop(
        0, block_total, gradient_step, initial
    )
    row_weight, row_points = lax.psum((row_weight, row_points), "tgt")
    source_gradient = 2.0 / epsilon * (row_weight[None, :] * source_points - row_points)
    column_weight, column_points = lax.psum((column_weight, column_points), "src")
    target_gradient = 2.0 / epsilon * (column_weight[None, :] * target_points - column_points)
    return (adjoint_source, adjoint_target, source_gradient, target_gradient)


def solution(mesh):
    return jax.shard_map(
        local,
        mesh=mesh,
        in_specs=(P(None, "src"), P("src"), P("src"), P(None, "tgt"), P("tgt"), P("tgt")),
        out_specs=(P("src"), P("tgt"), P(None, "src"), P(None, "tgt")),
        check_vma=False,
    )
```

profile of v0, /device:TPU:8, one launch (start us, length us, event | category | flops | bytes accessed | tf_op | source)
XLA Modules:
  0.0 2139.3 jit_solution(10395397590506230619)
XLA Ops:
  9.5 32.9 %while.52 = (s32[]{:T(128)}, f32[2,256]{1,0:T(2,128)S(1)}, f32[2,4096]{1,0:T(2,128)S(1)}, f32[2,4096]{1,0:T(2,128)S(1)}, f32[256]{0:T(256)S(1)}, /*index=5*/f32[...) while((s32[]{:T(128)}, f32[2,256]{1,0:T(2,128)S(1)}, ...), condition=%wide.region_6.0_spmd.clone, body=%wide.region_4.0_spmd.clone.sunk | while | flops 57573892 | bytes 1763545 | solution.py:113
  15.2 1.6 fusion.75
  19.3 1.6 fusion.75
  23.4 1.6 fusion.75
  27.5 1.6 fusion.75
  31.6 1.6 fusion.75
  35.7 1.6 fusion.75
  39.9 1.6 fusion.75
  42.3 443.4 %psum.86 = f32[2,4096]{1,0:T(2,128)S(1)} all-reduce(f32[2,4096]{1,0:T(2,128)S(1)} %get-tuple-element.547), channel_id=1, replica_groups=mesh['src'=64,'tgt'=8] {'src'}, use_global_device_ids=true, to_apply=%region_9.0 | all-reduce | flops 8192 | bytes 65536 | tf_op jit(solution)/shard_map/psum | solution.py:117
  487.7 10.9 psum.85
  500.5 95.8 %all-reduce.2 = (f32[]{:T(128)}, f32[]{:T(128)}) all-reduce(f32[]{:T(128)S(6)} %add.416, f32[]{:T(128)S(6)} %add.423), channel_id=1, replica_groups=mesh['src'=64,'tgt'=8] {'src','tgt'}, use_global_device_ids=true, to_apply=%region_2.0 | all-reduce | flops 2 | bytes 16 | tf_op jit(solution)/shard_map/psum | solution.py:70
  600.3 95.4 %psum.88 = f32[]{:T(128)} all-reduce(f32[]{:T(128)S(6)} %add.424), channel_id=1, replica_groups=mesh['src'=64,'tgt'=8] {'src','tgt'}, use_global_device_ids=true, to_apply=%region_14.0 | all-reduce | flops 1 | bytes 8 | tf_op jit(solution)/shard_map/psum | solution.py:70
  697.1 32.9 %while.53 = (s32[]{:T(128)}, f32[1,256]{1,0:T(1,128)S(1)}, f32[1,4096]{1,0:T(1,128)S(1)}, f32[1,4096]{1,0:T(1,128)S(1)}, f32[256]{0:T(256)S(1)}, /*index=5*/f32[...) while((s32[]{:T(128)}, f32[1,256]{1,0:T(1,128)S(1)}, ...), condition=%wide.region_17.0_spmd.clone, body=%wide.region_15.0_spmd.clone.sunk | while | flops 54427652 | bytes 1756377 | solution.py:113
  698.7 1.6 fusion.83
  719.2 1.6 fusion.83
  727.5 1.6 fusion.83
  729.9 431.4 %psum.90 = f32[4096]{0:T(1024)S(1)} all-reduce(f32[4096]{0:T(1024)S(1)} %bitcast.125), channel_id=1, replica_groups=mesh['src'=64,'tgt'=8] {'src'}, use_global_device_ids=true, to_apply=%region_20.0 | all-reduce | flops 4096 | bytes 32768 | tf_op jit(solution)/shard_map/psum | solution.py:117
  1162.6 12.4 psum.89
  1176.2 95.8 %psum.91 = f32[]{:T(128)} all-reduce(f32[]{:T(128)S(6)} %add.429), channel_id=1, replica_groups=mesh['src'=64,'tgt'=8] {'src','tgt'}, use_global_device_ids=true, to_apply=%region_22.0 | all-reduce | flops 1 | bytes 8 | tf_op jit(solution)/shard_map/psum | solution.py:123
  1273.5 24.5 %while.54 = (s32[]{:T(128)}, f32[256]{0:T(256)S(1)}, f32[32,256]{1,0:T(8,128)S(1)}, f32[4096]{0:T(1024)S(1)}, f32[32,4096]{1,0:T(8,128)S(1)}, /*index=5*/f32[256...) while((s32[]{:T(128)}, f32[256]{0:T(256)S(1)}, ...), condition=%wide.region_27.0_spmd.clone, body=%wide.region_23.0_spmd.clone.sunk | while | flops 152485120 | bytes 1996018 | solution.py:168
  1298.8 432.7 %psum.94 = f32[4096]{0:T(1024)S(1)} all-reduce(f32[4096]{0:T(1024)S(1)} %get-tuple-element.552), channel_id=1, replica_groups=mesh['src'=64,'tgt'=8] {'src'}, use_global_device_ids=true, to_apply=%region_30.0 | all-reduce | flops 4096 | bytes 32768 | tf_op jit(solution)/shard_map/psum | solution.py:173
  1731.5 24.6 %all-reduce.3 = (f32[32,256]{1,0:T(8,128)S(1)}, f32[256]{0:T(256)S(1)}) all-reduce(f32[32,256]{1,0:T(8,128)S(1)} %get-tuple-element.551, f32[256]{0:T(256)S(1)} %get-tuple-element.550), channel_id=1, replica_groups=mesh['src'=64,'tgt'=8] {'tgt'}, use_global_device_ids=true, to_apply=%region_29.0 | all-reduce | flops 8448 | bytes 67584 | tf_op jit(solution)/shard_map/psum | solution.py:171
  1756.7 373.9 %all-reduce.6.cloned.1.call-done = f32[32,4096]{1,0:T(8,128)} async-done(((f32[32,4096]{1,0:T(8,128)}), f32[32,4096]{1,0:T(8,128)}) %all-reduce.6.cloned.1.call-update) | async-done | bytes 524304 | tf_op jit(solution)/shard_map/psum | solution.py:173
  2130.6 1.9 subtract_multiply_fusion
  (176 shorter events, 81.4 us)
Async XLA Ops:
  7.2 2123.4 %all-reduce.6.cloned.1.call-start = ((), (), s32[]{:S(2)}) async-start(), calls=%async_computation | async-start | bytes 1048576 | tf_op jit(solution)/shard_map/psum | solution.py:173
  7.2 1.5 copy-start.3
  8.0 0.7 copy-start.5
  8.7 0.8 copy-start.2
  8.7 0.7 copy-start.7
  729.9 543.5 %copy-start = (f32[32,4096]{1,0:T(8,128)S(1)}, f32[32,4096]{1,0:T(8,128)}, u32[]{:S(2)}) copy-start(f32[32,4096]{1,0:T(8,128)} %get-tuple-element.1073) | copy-start | bytes 1572868
  1297.9 0.8 copy-start.1
  1298.0 0.8 copy-start.4
  1298.0 0.8 copy-start.6
Sparse Core Ops, SparseCore 0:
  1298.9 831.6 all-reduce.5
where the time goes:
time: 2140 us
  blocking collectives  1640 us (77%)
  waiting for transfers between devices  374 us (17%)
  matrix products  54.3 us (3%)
  local copies, waits for them, and re-layouts  23.5 us (1%)
  between operations  23.5 us (1%)
    psum x2, blocking collectives, local(): operator_column_total = lax.psum(operator_column_total, 'src')  875 us
    psum x1, blocking collectives, local(): lax.psum((column_weight, column_points), 'src')  433 us
    psum x1, waiting for transfers between devices, local(): lax.psum((column_weight, column_points), 'src')  374 us
    psum x2, blocking collectives, squared_norm(): lax.psum(local_inner(vector_source, vector_source, vector_target, vector_...  191 us
    psum x1, blocking collectives, local(): lax.psum(local_inner(direction_source, image_source, direction_target, im...  95.8 us
  transfers between devices with their start and end apart: 1, of which 1 were waited for; matrix products, arithmetic and copies ran while one was open for 0% of the time, Pallas kernels for 0%

commit v1 on v0

v1 whole, which is shorter than its diff:
```python
import functools
import math

import jax
import jax.numpy as jnp
from jax import lax
from jax.experimental import pallas as pl
from jax.experimental.pallas import tpu as pltpu
from jax.sharding import PartitionSpec as P

MESH = pl.DeviceIdType.MESH
F32 = jnp.float32
BF16 = jnp.bfloat16

NX, NY, NZ, NTG = 4, 2, 8, 8
NYZ = NY * NZ

D = 32
ROWS = 256
COLS = 4096
CHUNK = 512
RIDGE = 0.5
LOG2E = 1.4426950408889634
EXTRA = 512


def split2(v):
    high = v.astype(BF16)
    return high, (v - high.astype(F32)).astype(BF16)


def split3(v):
    high = v.astype(BF16)
    rest = v - high.astype(F32)
    mid = rest.astype(BF16)
    return high, mid, (rest - mid.astype(F32)).astype(BF16)


def dot_nn(a, b):
    return lax.dot_general(a, b, (((1,), (0,)), ((), ())), preferred_element_type=F32)


def dot_nt(a, b):
    return lax.dot_general(a, b, (((1,), (1,)), ((), ())), preferred_element_type=F32)


def dot_tn(a, b):
    return lax.dot_general(a, b, (((0,), (0,)), ((), ())), preferred_element_type=F32)


def kernel(
    factor_log2,
    xs_ref, xpot_ref, xcot_ref, ys_ref, ypot_ref, ycot_ref,
    sadj_ref, tadj_ref, sgrad_ref, tgrad_ref,
    bk, ph, pl_, colcrit, work, ubuf, wbuf,
    t1s, t1r, a1s, a1r, a1m, a1q, a2s, a2r, a2m, a2q,
    gc, gv, rxc, rxv, hc, hv, ryc, ryv,
    t2s, t2r, t3s, t3r, ag,
    send, recv,
):
    src = lax.axis_index("src")
    tgt = lax.axis_index("tgt")
    x = src // NYZ
    y = (src // NZ) % NY
    z = src % NZ

    def at(dx=0, dy=0, dz=0, dt=0):
        there = ((x + dx) % NX) * NYZ + ((y + dy) % NY) * NZ + (z + dz) % NZ
        return (there, (tgt + dt) % NTG)

    def post(source, target, sem, peer):
        pltpu.make_async_remote_copy(
            src_ref=source, dst_ref=target, send_sem=send.at[sem], recv_sem=recv.at[sem],
            device_id=peer, device_id_type=MESH,
        ).start()

    def arrive(ref, sem):
        pltpu.make_async_copy(ref, ref, recv.at[sem]).wait()

    z_peers = [dict(dz=k) for k in range(1, NZ)]
    xy_peers = [dict(dx=k // NY, dy=k % NY) for k in range(1, NX * NY)]
    yz_peers = [dict(dy=k // NZ, dz=k % NZ) for k in range(1, NYZ)]
    x_peers = [dict(dx=k) for k in range(1, NX)]
    t_peers = [dict(dt=k) for k in range(1, NTG)]

    barrier = pltpu.get_barrier_semaphore()
    greet = t_peers + yz_peers + [p for p in xy_peers if p["dx"]]
    for p in greet:
        pl.semaphore_signal(barrier, inc=1, device_id=at(**p), device_id_type=MESH)

    xs = xs_ref[...]
    cs = xcot_ref[...]
    ct = ycot_ref[...]
    x1, x2, x3 = split3(xs * (4.0 * LOG2E))
    row_term = (xpot_ref[...] - 2.0 * jnp.sum(xs * xs, axis=0, keepdims=True)) * LOG2E
    r1, r2, r3 = split3(row_term)
    one_r = jnp.ones((1, ROWS), F32)
    tail_a = jnp.concatenate(
        [r1.astype(F32), r2.astype(F32), r3.astype(F32), one_r, one_r, one_r,
         jnp.zeros((26, ROWS), F32)], axis=0,
    ).astype(BF16)
    ak = jnp.concatenate([x1, x1, x2, x2, x1, x3, tail_a], axis=0)

    ones_crit = jnp.ones((1, ROWS), F32)
    cs_h, cs_l = split2(cs)
    s_crit = jnp.concatenate(
        [ones_crit, cs_h.astype(F32), cs_l.astype(F32), jnp.zeros((13, ROWS), F32)], axis=0
    ).astype(BF16)

    def build(i, row_acc):
        at_c = pl.ds(pl.multiple_of(i * CHUNK, CHUNK), CHUNK)
        yc = ys_ref[:, at_c]
        y1, y2, y3 = split3(yc)
        col_term = (ypot_ref[:, at_c] - 2.0 * jnp.sum(yc * yc, axis=0, keepdims=True)) * LOG2E
        c1, c2, c3 = split3(col_term + factor_log2)
        one_c = jnp.ones((1, CHUNK), F32)
        tail_b = jnp.concatenate(
            [one_c, one_c, one_c, c1.astype(F32), c2.astype(F32), c3.astype(F32),
             jnp.zeros((26, CHUNK), F32)], axis=0,
        ).astype(BF16)
        bk[...] = jnp.concatenate([y1, y2, y1, y2, y3, y1, tail_b], axis=0)
        plan = jnp.exp2(dot_tn(ak, bk[...]))
        high, low = split2(plan)
        ph[:, at_c] = high
        pl_[:, at_c] = low
        colcrit[:, at_c] = dot_nn(s_crit, high) + dot_nn(s_crit, low)
        ct_h, ct_l = split2(ct_at(at_c))
        t_crit = jnp.concatenate(
            [one_c, ct_h.astype(F32), ct_l.astype(F32), jnp.zeros((13, CHUNK), F32)], axis=0
        ).astype(BF16)
        return row_acc + dot_nt(t_crit, high) + dot_nt(t_crit, low)

    def ct_at(at_c):
        return ycot_ref[:, at_c]

    row_crit = lax.fori_loop(0, COLS // CHUNK, build, jnp.zeros((16, ROWS), F32))
    rm_part = row_crit[0:1]
    pct_part = row_crit[1:2] + row_crit[2:3]
    cm_part = colcrit[0:1, :]
    pcs_part = colcrit[1:2, :] + colcrit[2:3, :]

    pl.semaphore_wait(barrier, len(greet))

    t1s[...] = jnp.concatenate([rm_part, pct_part], axis=1)
    a1s[...] = cm_part * ct + pcs_part
    for i, p in enumerate(t_peers):
        post(t1s, t1r.at[i], 0, at(**p))
    for i, p in enumerate(z_peers):
        post(a1s, a1r.at[i], 1, at(**p))

    def col_products(vectors, width):
        high, low = split2(vectors)
        stack = jnp.concatenate([high, low], axis=0)

        def step(i, c):
            at_c = pl.ds(pl.multiple_of(i * CHUNK, CHUNK), CHUNK)
            r = dot_nn(stack, ph[:, at_c]) + dot_nn(stack, pl_[:, at_c])
            work[0:width, at_c] = r[:width] + r[width:]
            return c

        lax.fori_loop(0, COLS // CHUNK, step, 0)

    def row_products(make, width):
        def step(i, acc):
            at_c = pl.ds(pl.multiple_of(i * CHUNK, CHUNK), CHUNK)
            high, low = split2(make(at_c))
            stack = jnp.concatenate([high, low], axis=0)
            r = dot_nt(stack, ph[:, at_c]) + dot_nt(stack, pl_[:, at_c])
            return acc + r[:width] + r[width:]

        return lax.fori_loop(0, COLS // CHUNK, step, jnp.zeros((width, ROWS), F32))

    def place(o):
        ox, oy, oz = o // NYZ, (o // NZ) % NY, o % NZ
        return ((ox - x + NX) % NX) * NYZ + ((oy - y + NY) % NY) * NZ + (oz - z + NZ) % NZ

    col_products(jnp.concatenate([xs, xs * cs], axis=0), 64)
    for c in range(COLS // 128):
        lanes = slice(c * 128, c * 128 + 128)
        yc = ys_ref[:, lanes]
        u = colcrit[0:1, lanes] * yc - work[0:32, lanes]
        ubuf[:, lanes] = u
        g = ycot_ref[:, lanes] * u + pcs_part[:, lanes] * yc - work[32:64, lanes]
        gc[place(2 * c)] = g[0:16]
        gc[place(2 * c + 1)] = g[16:32]

    arrive(t1r, 0)
    rows_sum = t1s[...]
    for i in range(NTG - 1):
        rows_sum = rows_sum + t1r[i]
    rm = rows_sum[:, :ROWS]
    vs = rm * cs + rows_sum[:, ROWS:]
    col_products(jnp.concatenate([xs * vs, vs, jnp.zeros((15, ROWS), F32)], axis=0), 48)
    pvs_part = work[32:33, :]
    a2s[...] = jnp.concatenate(
        [
            jnp.concatenate([pvs_part, cs * cs, cs * vs], axis=1),
            jnp.concatenate([cm_part, vs * vs, rm * vs * vs], axis=1),
        ],
        axis=0,
    )

    arrive(a1r, 1)
    total = a1s[...]
    for i in range(NZ - 1):
        total = total + a1r[i]
    a1m[...] = total
    for i, p in enumerate(xy_peers):
        post(a1m, a1q.at[i], 2, at(**p))
    for i, p in enumerate(z_peers):
        post(a2s, a2r.at[i], 3, at(**p))

    def post_x(buf, into, base):
        for g in (3, 2, 1, 0):
            for m in range(1, NX):
                post(buf.at[pl.ds(m * NYZ + 4 * g, 4)], into.at[g, m - 1], base + g, at(dx=m))

    post_x(gc, rxc, 8)

    for c in range(COLS // 128):
        lanes = slice(c * 128, c * 128 + 128)
        wbuf[:, lanes] = work[32:33, lanes] * ys_ref[:, lanes] - work[0:32, lanes]

    def make_c(at_c):
        yc = ys_ref[:, at_c]
        return jnp.concatenate([yc, yc * ct_at(at_c)], axis=0)

    rp = row_products(make_c, 64)
    row_u = rm_part * xs - rp[0:32]
    t2s[0] = cs * row_u + pct_part * xs - rp[32:64]
    for i, p in enumerate(t_peers):
        post(t2s.at[0], t2r.at[0, i], 4, at(**p))

    arrive(a2r, 3)
    total2 = a2s[...]
    for i in range(NZ - 1):
        total2 = total2 + a2r[i]
    a2m[...] = total2
    for i, p in enumerate(xy_peers):
        post(a2m, a2q.at[i], 5, at(**p))

    arrive(a1q, 2)
    vt = a1m[...]
    for i in range(NX * NY - 1):
        vt = vt + a1q[i]
    for c in range(COLS // 128):
        lanes = slice(c * 128, c * 128 + 128)
        g = vt[:, lanes] * ubuf[:, lanes] + wbuf[:, lanes]
        gv[place(2 * c)] = g[0:16]
        gv[place(2 * c + 1)] = g[16:32]
    post_x(gv, rxv, 12)
    tadj_ref[...] = vt

    def make_v(at_c):
        v = tadj_ref[:, at_c]
        return jnp.concatenate([ys_ref[:, at_c] * v, v, jnp.zeros((15, CHUNK), F32)], axis=0)

    rp = row_products(make_v, 48)
    t2s[1] = vs * row_u + rp[32:33] * xs - rp[0:32]
    for i, p in enumerate(t_peers):
        post(t2s.at[1], t2r.at[1, i], 6, at(**p))

    def add_x(buf, inbox, held, outbox, base, sem):
        for g in (3, 2, 1, 0):
            arrive(inbox.at[g], base + g)
            for s in range(4 * g, 4 * g + 4):
                held[s] = buf[s] + inbox[g, 0, s - 4 * g] + inbox[g, 1, s - 4 * g] + inbox[g, 2, s - 4 * g]
            for s in range(4 * g, 4 * g + 4):
                if s:
                    post(held.at[s], outbox.at[s - 1], sem, at(dy=s // NZ, dz=s % NZ))

    add_x(gc, rxc, hc, ryc, 8, 16)
    add_x(gv, rxv, hv, ryv, 12, 17)

    arrive(a2q, 5)
    total2 = a2m[...]
    for i in range(NX * NY - 1):
        total2 = total2 + a2q[i]
    pvs = total2[0:1, :COLS]
    cm = total2[1:2, :COLS]
    over_src = [
        total2[0:1, COLS : COLS + 256],
        total2[0:1, COLS + 256 :],
        total2[1:2, COLS : COLS + 256],
        total2[1:2, COLS + 256 :],
    ]

    def fold(v):
        acc = v[:, 0:128]
        for c in range(1, COLS // 128):
            acc = acc + v[:, c * 128 : c * 128 + 128]
        return acc

    t3s[...] = jnp.concatenate(
        [fold(ct * ct), fold(ct * vt), fold(vt * vt), fold(vt * (cm * vt + 2.0 * pvs))], axis=1
    )
    for i, p in enumerate(t_peers):
        post(t3s, t3r.at[i], 7, at(**p))
    arrive(t3r, 7)
    over_tgt = t3s[...]
    for i in range(NTG - 1):
        over_tgt = over_tgt + t3r[i]
    m0, g1, g2, g3 = (
        jnp.sum(a[:, 0:128] + a[:, 128:256] + over_tgt[:, q * 128 : q * 128 + 128], axis=1, keepdims=True)
        for q, a in enumerate(over_src)
    )
    mu = g1 / m0
    h2 = jnp.maximum(g2 - g1 * mu, 0.0)
    h3 = g3 - 2.0 * mu * g2 + mu * mu * g1
    step0 = 1.0 / (RIDGE + mu)
    below = RIDGE * h2 + h3 - step0 * h2 * h2 / m0
    step1 = h2 / jnp.maximum(jnp.maximum(below, RIDGE * h2), 1e-37)
    beta = step0 * step0 * h2 / m0
    of_c = step0 + step1 * (beta + step0 * mu)
    of_v = -(step0 * step1)

    sadj_ref[...] = of_c * cs + of_v * vs
    tadj_ref[...] = of_c * ct + of_v * vt
    k_c = 4.0 * of_c
    k_v = 4.0 * of_v

    arrive(ryc, 16)
    piece_c = hc[0]
    for s in range(NYZ - 1):
        piece_c = piece_c + ryc[s]
    arrive(ryv, 17)
    piece_v = hv[0]
    for s in range(NYZ - 1):
        piece_v = piece_v + ryv[s]
    ag[0, 0] = k_c * piece_c + k_v * piece_v
    for s in range(NYZ - 1, 0, -1):
        post(ag.at[0, 0], ag.at[0, s], 18 + s // 4, at(dy=s // NZ, dz=s % NZ))

    arrive(t2r.at[0], 4)
    arrive(t2r.at[1], 6)
    grad_c, grad_v = t2s[0], t2s[1]
    for i in range(NTG - 1):
        grad_c = grad_c + t2r[0, i]
        grad_v = grad_v + t2r[1, i]
    sgrad_ref[...] = k_c * grad_c + k_v * grad_v

    for g in range(4):
        arrive(ag.at[0, pl.ds(max(4 * g, 1), 4 if g else 3)], 18 + g)
        for m in range(1, NX):
            post(ag.at[0, pl.ds(4 * g, 4)], ag.at[m, pl.ds(4 * g, 4)], 22, at(dx=m))
    arrive(ag.at[pl.ds(1, 3)], 22)

    for c in range(COLS // 128):
        for h in range(2):
            o = 2 * c + h
            ox, oy, oz = o // NYZ, (o // NZ) % NY, o % NZ
            slot = ((y - oy + NY) % NY) * NZ + (z - oz + NZ) % NZ
            tgrad_ref[16 * h : 16 * h + 16, c * 128 : c * 128 + 128] = ag[(x - ox + NX) % NX, slot]

    def sent(ref, sem):
        pltpu.make_async_copy(ref, ref, send.at[sem]).wait()

    sent(t1r, 0)
    sent(a1r, 1)
    sent(a1q, 2)
    sent(a2r, 3)
    sent(t2r.at[0], 4)
    sent(a2q, 5)
    sent(t2r.at[1], 6)
    sent(t3r, 7)
    for g in range(4):
        sent(rxc.at[g], 8 + g)
        sent(rxv.at[g], 12 + g)
        sent(ag.at[0, pl.ds(max(4 * g, 1), 4 if g else 3)], 18 + g)
    sent(ryc, 16)
    sent(ryv, 17)
    sent(ag.at[pl.ds(1, 3)], 22)


def solution(mesh):
    def local(xs, xpot, xcot, ys, ypot, ycot):
        count = xs.shape[1] * mesh.shape["src"] * ys.shape[1] * mesh.shape["tgt"]
        vmem = pl.BlockSpec(memory_space=pltpu.VMEM)
        sadj, tadj, sgrad, tgrad = pl.pallas_call(
            functools.partial(kernel, -0.5 * math.log2(count)),
            out_shape=(
                jax.ShapeDtypeStruct((1, ROWS), F32),
                jax.ShapeDtypeStruct((1, COLS), F32),
                jax.ShapeDtypeStruct((D, ROWS), F32),
                jax.ShapeDtypeStruct((D, COLS), F32),
            ),
            in_specs=[vmem] * 6,
            out_specs=(vmem,) * 4,
            scratch_shapes=[
                pltpu.VMEM((224, CHUNK), BF16),
                pltpu.VMEM((ROWS, COLS), BF16),
                pltpu.VMEM((ROWS, COLS), BF16),
                pltpu.VMEM((16, COLS), F32),
                pltpu.VMEM((64, COLS), F32),
                pltpu.VMEM((D, COLS), F32),
                pltpu.VMEM((D, COLS), F32),
                pltpu.VMEM((1, 2 * ROWS), F32),
                pltpu.VMEM((NTG - 1, 1, 2 * ROWS), F32),
                pltpu.VMEM((1, COLS), F32),
                pltpu.VMEM((NZ - 1, 1, COLS), F32),
                pltpu.VMEM((1, COLS), F32),
                pltpu.VMEM((NX * NY - 1, 1, COLS), F32),
                pltpu.VMEM((2, COLS + EXTRA), F32),
                pltpu.VMEM((NZ - 1, 2, COLS + EXTRA), F32),
                pltpu.VMEM((2, COLS + EXTRA), F32),
                pltpu.VMEM((NX * NY - 1, 2, COLS + EXTRA), F32),
                pltpu.VMEM((NX * NYZ, 16, 128), F32),
                pltpu.VMEM((NX * NYZ, 16, 128), F32),
                pltpu.VMEM((4, NX - 1, 4, 16, 128), F32),
                pltpu.VMEM((4, NX - 1, 4, 16, 128), F32),
                pltpu.VMEM((NYZ, 16, 128), F32),
                pltpu.VMEM((NYZ, 16, 128), F32),
                pltpu.VMEM((NYZ - 1, 16, 128), F32),
                pltpu.VMEM((NYZ - 1, 16, 128), F32),
                pltpu.VMEM((2, D, ROWS), F32),
                pltpu.VMEM((2, NTG - 1, D, ROWS), F32),
                pltpu.VMEM((1, 512), F32),
                pltpu.VMEM((NTG - 1, 1, 512), F32),
                pltpu.VMEM((NX, NYZ, 16, 128), F32),
                pltpu.SemaphoreType.DMA((23,)),
                pltpu.SemaphoreType.DMA((23,)),
            ],
            compiler_params=pltpu.CompilerParams(
                collective_id=0, has_side_effects=True, vmem_limit_bytes=48 * 2**20
            ),
        )(xs, xpot.reshape(1, ROWS), xcot.reshape(1, ROWS), ys, ypot.reshape(1, COLS), ycot.reshape(1, COLS))
        return sadj.reshape(ROWS), tadj.reshape(COLS), sgrad, tgrad

    return jax.shard_map(
        local,
        mesh=mesh,
        in_specs=(P(None, "src"), P("src"), P("src"), P(None, "tgt"), P("tgt"), P("tgt")),
        out_specs=(P("src"), P("tgt"), P(None, "src"), P(None, "tgt")),
        check_vma=False,
    )
```

time: 2140 us -> 72.9 us (0.03)
  the two profiles are of different devices: /device:TPU:8 before, /device:TPU:1 now
where the time goes in v1:
time: 72.9 us; the launch traced here: 72.6 us
  Pallas kernels  65.4 us (90%)
  local copies, waits for them, and re-layouts  6.49 us (9%)
    pallas_call x1, Pallas kernels, local(): pl.pallas_call(functools.partial(kernel, -0.5 * math.log2(count)), out_sh...  65.4 us
    unnamed x16, local copies, waits for them, and re-layouts  6.49 us

profile of v1, /device:TPU:1, one launch (start us, length us, event | category | flops | bytes accessed | tf_op | source)
XLA Modules:
  0.0 72.6 jit_solution(3516829561158596888)
XLA Ops:
  0.6 0.0 copy-start.5
  0.6 0.0 copy-start.4
  0.7 0.7 copy-done.5
  1.3 0.0 copy-done.4
  1.3 0.0 copy-start
  1.3 1.0 %copy-done = f32[32,4096]{1,0:T(8,128)S(1)} copy-done((f32[32,4096]{1,0:T(8,128)S(1)}, f32[32,4096]{1,0:T(8,128)}, u32[]{:S(2)}) %copy-start) | copy-done | bytes 524312
  2.4 0.0 copy-start.1
  2.4 0.8 %copy-done.1 = f32[32,256]{1,0:T(8,128)S(1)} copy-done((f32[32,256]{1,0:T(8,128)S(1)}, f32[32,256]{1,0:T(8,128)}, u32[]{:S(2)}) %copy-start.1) | copy-done | bytes 32792
  3.1 0.0 copy-start.2
  3.1 0.7 copy-done.2
  3.8 0.0 copy-start.3
  3.8 0.7 copy-done.3
  4.6 65.4 %shard_map.93 = (f32[1,256]{1,0:T(1,128)S(1)}, f32[1,4096]{1,0:T(1,128)S(1)}, f32[32,256]{1,0:T(8,128)S(1)}, f32[32,4096]{1,0:T(8,128)S(1)}) custom-call(f32[32,256]{1,0:T(8,128)S(1)} %copy-done.1, f32[1,256]{1,0:T(1,128)S(1)} %bitcast.9, f32[1,256]{1,0:T(1,128)S(1)} %bitcast.10, f32[32,4096]{1,0:T(8,128)S(1)} %copy-done, f32[1,4096]{1,0:T(1,128)S(1)} %bitcast.6, ...), custom_call_target="tpu_custom_call" | custom-call | tf_op jit(solution)/shard_map/pallas_call | solution.py:379
  70.0 0.6 copy.14
  70.6 0.6 copy.15
  71.2 0.6 copy.16
  71.8 0.8 %copy.17 = f32[32,4096]{1,0:T(8,128)} copy(f32[32,4096]{1,0:T(8,128)S(1)} %get-tuple-element.19) | data formatting | bytes 1048576
Async XLA Ops:
  0.6 0.7 copy-start.5
  0.6 0.7 copy-start.4
  1.3 1.0 %copy-start = (f32[32,4096]{1,0:T(8,128)S(1)}, f32[32,4096]{1,0:T(8,128)}, u32[]{:S(2)}) copy-start(f32[32,4096]{1,0:T(8,128)} %ys_ref.1) | copy-start | bytes 1572868
  2.4 0.8 %copy-start.1 = (f32[32,256]{1,0:T(8,128)S(1)}, f32[32,256]{1,0:T(8,128)}, u32[]{:S(2)}) copy-start(f32[32,256]{1,0:T(8,128)} %xs_ref.1) | copy-start | bytes 98308
  3.1 0.7 copy-start.2
  3.8 0.7 copy-start.3

commit v2 on v1

v2 whole, which is shorter than its diff:
```python
import functools
import math

import jax
import jax.numpy as jnp
from jax import lax
from jax.experimental import pallas as pl
from jax.experimental.pallas import tpu as pltpu
from jax.sharding import PartitionSpec as P

MESH = pl.DeviceIdType.MESH
F32 = jnp.float32
BF16 = jnp.bfloat16

NX, NY, NZ, NTG = 4, 2, 8, 8
NYZ = NY * NZ

D = 32
ROWS = 256
COLS = 4096
CHUNK = 512
RIDGE = 0.5
LOG2E = 1.4426950408889634


def split2(v):
    high = v.astype(BF16)
    return high, (v - high.astype(F32)).astype(BF16)


def split3(v):
    high = v.astype(BF16)
    rest = v - high.astype(F32)
    mid = rest.astype(BF16)
    return high, mid, (rest - mid.astype(F32)).astype(BF16)


def dot_nn(a, b):
    return lax.dot_general(a, b, (((1,), (0,)), ((), ())), preferred_element_type=F32)


def dot_nt(a, b):
    return lax.dot_general(a, b, (((1,), (1,)), ((), ())), preferred_element_type=F32)


def dot_tn(a, b):
    return lax.dot_general(a, b, (((0,), (0,)), ((), ())), preferred_element_type=F32)


def kernel(
    factor_log2,
    xs_hbm, xpot_hbm, xcot_hbm, ys_hbm, ypot_hbm, ycot_hbm,
    sadj_hbm, tadj_hbm, sgrad_hbm, tgrad_hbm,
    xs_ref, xpot_ref, xcot_ref, ys_ref, ypot_ref, ycot_ref,
    sadj_ref, tadj_ref, sgrad_ref, tgrad_ref,
    bk, ph, pl_, cm_ref, pcs_ref, work, ubuf, wbuf,
    t1s, t1r, a1s, a1r, a1m, a1q,
    gc, gv, rxc, rxv, hc, hv, ryc, ryv,
    t2s, t2r, t4, qs, qr, qm, qq, ag,
    load, store, send, recv,
):
    loads = [
        pltpu.make_async_copy(a, b, load.at[i])
        for i, (a, b) in enumerate(
            [(xs_hbm, xs_ref), (xpot_hbm, xpot_ref), (xcot_hbm, xcot_ref),
             (ypot_hbm, ypot_ref), (ycot_hbm, ycot_ref)]
            + [(ys_hbm.at[:, pl.ds(k * 1024, 1024)], ys_ref.at[:, pl.ds(k * 1024, 1024)]) for k in range(4)]
        )
    ]
    for c in loads:
        c.start()
    src = lax.axis_index("src")
    tgt = lax.axis_index("tgt")
    x = src // NYZ
    y = (src // NZ) % NY
    z = src % NZ

    def at(dx=0, dy=0, dz=0, dt=0):
        there = ((x + dx) % NX) * NYZ + ((y + dy) % NY) * NZ + (z + dz) % NZ
        return (there, (tgt + dt) % NTG)

    def post(source, target, sem, peer):
        pltpu.make_async_remote_copy(
            src_ref=source, dst_ref=target, send_sem=send.at[sem], recv_sem=recv.at[sem],
            device_id=peer, device_id_type=MESH,
        ).start()

    def arrive(ref, sem):
        pltpu.make_async_copy(ref, ref, recv.at[sem]).wait()

    z_peers = [dict(dz=k) for k in range(1, NZ)]
    xy_peers = [dict(dx=k // NY, dy=k % NY) for k in range(1, NX * NY)]
    yz_peers = [dict(dy=k // NZ, dz=k % NZ) for k in range(1, NYZ)]
    x_peers = [dict(dx=k) for k in range(1, NX)]
    t_peers = [dict(dt=k) for k in range(1, NTG)]
    tx_peers = [dict(dx=k // NTG, dt=k % NTG) for k in range(1, NX * NTG)]

    barrier = pltpu.get_barrier_semaphore()
    greet = tx_peers + yz_peers + [p for p in xy_peers if p["dx"] and p["dy"]]
    for p in greet:
        pl.semaphore_signal(barrier, inc=1, device_id=at(**p), device_id_type=MESH)

    for c in loads[:5]:
        c.wait()
    xs = xs_ref[...]
    cs = xcot_ref[...]
    ct = ycot_ref[...]
    x1, x2, x3 = split3(xs * (4.0 * LOG2E))
    row_term = (xpot_ref[...] - 2.0 * jnp.sum(xs * xs, axis=0, keepdims=True)) * LOG2E
    r1, r2, r3 = split3(row_term)
    one_r = jnp.ones((1, ROWS), F32)
    tail_a = jnp.concatenate(
        [r1.astype(F32), r2.astype(F32), r3.astype(F32), one_r, one_r, one_r,
         jnp.zeros((26, ROWS), F32)], axis=0,
    ).astype(BF16)
    ak = jnp.concatenate([x1, x1, x2, x2, x1, x3, tail_a], axis=0)

    ones_crit = jnp.ones((1, ROWS), F32)
    cs_h, cs_l = split2(cs)
    s_crit = jnp.concatenate(
        [ones_crit, cs_h.astype(F32), cs_l.astype(F32), jnp.zeros((13, ROWS), F32)], axis=0
    ).astype(BF16)

    row_crit = jnp.zeros((16, ROWS), F32)
    one_c = jnp.ones((1, CHUNK), F32)
    for i in range(COLS // CHUNK):
        if i * CHUNK % 1024 == 0:
            loads[5 + i * CHUNK // 1024].wait()
        at_c = slice(i * CHUNK, i * CHUNK + CHUNK)
        yc = ys_ref[:, at_c]
        ctc = ycot_ref[:, at_c]
        y1, y2, y3 = split3(yc)
        col_term = (ypot_ref[:, at_c] - 2.0 * jnp.sum(yc * yc, axis=0, keepdims=True)) * LOG2E
        c1, c2, c3 = split3(col_term + factor_log2)
        tail_b = jnp.concatenate(
            [one_c, one_c, one_c, c1.astype(F32), c2.astype(F32), c3.astype(F32),
             jnp.zeros((26, CHUNK), F32)], axis=0,
        ).astype(BF16)
        bk[i % 2] = jnp.concatenate([y1, y2, y1, y2, y3, y1, tail_b], axis=0)
        plan = jnp.exp2(dot_tn(ak, bk[i % 2]))
        high, low = split2(plan)
        ph[:, at_c] = high
        pl_[:, at_c] = low
        r = dot_nn(s_crit, high) + dot_nn(s_crit, low)
        cm_c = r[0:1]
        pcs_c = r[1:2] + r[2:3]
        cm_ref[:, at_c] = cm_c
        pcs_ref[:, at_c] = pcs_c
        a1s[:, at_c] = cm_c * ctc + pcs_c
        ct_h, ct_l = split2(ctc)
        t_crit = jnp.concatenate(
            [one_c, ct_h.astype(F32), ct_l.astype(F32), jnp.zeros((13, CHUNK), F32)], axis=0
        ).astype(BF16)
        row_crit = row_crit + dot_nt(t_crit, high) + dot_nt(t_crit, low)

    rm_part = row_crit[0:1]
    pct_part = row_crit[1:2] + row_crit[2:3]
    t1s[...] = jnp.concatenate([rm_part, pct_part], axis=1)

    pl.semaphore_wait(barrier, len(greet))

    for i, p in enumerate(t_peers):
        post(t1s, t1r.at[i], 0, at(**p))
    for i, p in enumerate(z_peers):
        post(a1s, a1r.at[i], 1, at(**p))

    def col_products(vectors, width):
        high, low = split2(vectors)
        stack = jnp.concatenate([high, low], axis=0)

        def step(i, c):
            at_c = pl.ds(pl.multiple_of(i * CHUNK, CHUNK), CHUNK)
            r = dot_nn(stack, ph[:, at_c]) + dot_nn(stack, pl_[:, at_c])
            work[0:width, at_c] = r[:width] + r[width:]
            return c

        lax.fori_loop(0, COLS // CHUNK, step, 0)

    def row_products(make, width):
        def step(i, acc):
            at_c = pl.ds(pl.multiple_of(i * CHUNK, CHUNK), CHUNK)
            high, low = split2(make(at_c))
            stack = jnp.concatenate([high, low], axis=0)
            r = dot_nt(stack, ph[:, at_c]) + dot_nt(stack, pl_[:, at_c])
            return acc + r[:width] + r[width:]

        return lax.fori_loop(0, COLS // CHUNK, step, jnp.zeros((width, ROWS), F32))

    def place(o):
        ox, oy, oz = o // NYZ, (o // NZ) % NY, o % NZ
        return ((ox - x + NX) % NX) * NYZ + ((oy - y + NY) % NY) * NZ + (oz - z + NZ) % NZ

    col_products(jnp.concatenate([xs, xs * cs], axis=0), 64)
    for c in range(COLS // 128):
        lanes = slice(c * 128, c * 128 + 128)
        yc = ys_ref[:, lanes]
        u = cm_ref[:, lanes] * yc - work[0:32, lanes]
        ubuf[:, lanes] = u
        g = ycot_ref[:, lanes] * u + pcs_ref[:, lanes] * yc - work[32:64, lanes]
        gc[place(2 * c)] = g[0:16]
        gc[place(2 * c + 1)] = g[16:32]

    def post_x(buf, into, base):
        for g in (3, 2, 1, 0):
            for m in range(1, NX):
                post(buf.at[pl.ds(m * NYZ + 4 * g, 4)], into.at[g, m - 1], base + g, at(dx=m))

    post_x(gc, rxc, 8)

    arrive(t1r, 0)
    rows_sum = t1s[...]
    for i in range(NTG - 1):
        rows_sum = rows_sum + t1r[i]
    rm = rows_sum[:, :ROWS]
    vs = rm * cs + rows_sum[:, ROWS:]
    col_products(jnp.concatenate([xs * vs, vs, jnp.zeros((15, ROWS), F32)], axis=0), 48)
    for c in range(COLS // 128):
        lanes = slice(c * 128, c * 128 + 128)
        wbuf[:, lanes] = work[32:33, lanes] * ys_ref[:, lanes] - work[0:32, lanes]

    arrive(a1r, 1)
    total = a1s[...]
    for i in range(NZ - 1):
        total = total + a1r[i]
    a1m[...] = total
    for i, p in enumerate(xy_peers):
        post(a1m, a1q.at[i], 2, at(**p))

    def make_c(at_c):
        yc = ys_ref[:, at_c]
        return jnp.concatenate([yc, yc * ycot_ref[:, at_c]], axis=0)

    rp = row_products(make_c, 64)
    row_u = rm_part * xs - rp[0:32]
    row_c = cs * row_u + pct_part * xs - rp[32:64]

    def add_x(buf, inbox, held, outbox, base, sem):
        for g in (3, 2, 1, 0):
            arrive(inbox.at[g], base + g)
            for s in range(4 * g, 4 * g + 4):
                held[s] = buf[s] + inbox[g, 0, s - 4 * g] + inbox[g, 1, s - 4 * g] + inbox[g, 2, s - 4 * g]
            for s in range(4 * g, 4 * g + 4):
                if s:
                    post(held.at[s], outbox.at[s - 1], sem, at(dy=s // NZ, dz=s % NZ))

    add_x(gc, rxc, hc, ryc, 8, 16)

    arrive(a1q, 2)
    vt = a1m[...]
    for i in range(NX * NY - 1):
        vt = vt + a1q[i]
    for c in range(COLS // 128):
        lanes = slice(c * 128, c * 128 + 128)
        g = vt[:, lanes] * ubuf[:, lanes] + wbuf[:, lanes]
        gv[place(2 * c)] = g[0:16]
        gv[place(2 * c + 1)] = g[16:32]
    post_x(gv, rxv, 12)
    tadj_ref[...] = vt

    def fold(v):
        acc = v[:, 0:128]
        for c in range(1, v.shape[1] // 128):
            acc = acc + v[:, c * 128 : c * 128 + 128]
        return acc

    of_src, of_tgt = 1.0 / NTG, 1.0 / (NX * NYZ)
    ct = ycot_ref[...]
    pvs_part = work[32:33, :]
    qs[...] = jnp.concatenate(
        [
            fold(cs * cs) * of_src + fold(ct * ct) * of_tgt,
            fold(cs * vs) * of_src + fold(ct * vt) * of_tgt,
            fold(vs * vs) * of_src + fold(vt * vt) * of_tgt,
            fold(rm_part * vs * vs) + fold(vt * (cm_ref[...] * vt + 2.0 * pvs_part)),
        ],
        axis=1,
    )
    for i, p in enumerate(tx_peers):
        post(qs, qr.at[i], 3, at(**p))

    def make_v(at_c):
        v = tadj_ref[:, at_c]
        return jnp.concatenate([ys_ref[:, at_c] * v, v, jnp.zeros((15, CHUNK), F32)], axis=0)

    rp = row_products(make_v, 48)
    row_v = vs * row_u + rp[32:33] * xs - rp[0:32]
    for p in range(NTG):
        rows, lanes = slice(p // 2 * 8, p // 2 * 8 + 8), slice(p % 2 * 128, p % 2 * 128 + 128)
        slot = (p - tgt + NTG) % NTG
        t2s[slot, 0] = row_c[rows, lanes]
        t2s[slot, 1] = row_v[rows, lanes]
    for i, p in enumerate(t_peers):
        post(t2s.at[i + 1], t2r.at[i], 4, at(**p))

    add_x(gv, rxv, hv, ryv, 12, 17)

    arrive(qr, 3)
    inner = qs[...]
    for i in range(NX * NTG - 1):
        inner = inner + qr[i]
    qm[...] = inner
    for i, p in enumerate(yz_peers):
        post(qm, qq.at[i], 5, at(**p))

    arrive(ryc, 16)
    piece_c = hc[0]
    for s in range(NYZ - 1):
        piece_c = piece_c + ryc[s]
    arrive(t2r, 4)
    row_piece = t2s[0]
    for i in range(NTG - 1):
        row_piece = row_piece + t2r[i]

    arrive(qq, 5)
    inner = qm[...]
    for i in range(NYZ - 1):
        inner = inner + qq[i]
    m0, g1, g2, g3 = (
        jnp.sum(inner[:, q * 128 : q * 128 + 128], axis=1, keepdims=True) for q in range(4)
    )
    mu = g1 / m0
    h2 = jnp.maximum(g2 - g1 * mu, 0.0)
    h3 = g3 - 2.0 * mu * g2 + mu * mu * g1
    step0 = 1.0 / (RIDGE + mu)
    below = RIDGE * h2 + h3 - step0 * h2 * h2 / m0
    step1 = h2 / jnp.maximum(jnp.maximum(below, RIDGE * h2), 1e-37)
    beta = step0 * step0 * h2 / m0
    of_c = step0 + step1 * (beta + step0 * mu)
    of_v = -(step0 * step1)

    k_c = 4.0 * of_c
    k_v = 4.0 * of_v

    arrive(ryv, 17)
    piece_v = hv[0]
    for s in range(NYZ - 1):
        piece_v = piece_v + ryv[s]
    ag[0, 0] = k_c * piece_c + k_v * piece_v
    for s in range(NYZ - 1, 0, -1):
        post(ag.at[0, 0], ag.at[0, s], 18 + s // 4, at(dy=s // NZ, dz=s % NZ))

    t4[0] = k_c * row_piece[0] + k_v * row_piece[1]
    for i, p in enumerate(t_peers):
        post(t4.at[0], t4.at[i + 1], 6, at(**p))
    sadj_ref[...] = of_c * cs + of_v * vs
    tadj_ref[...] = of_c * ct + of_v * vt
    stores = [
        pltpu.make_async_copy(sadj_ref, sadj_hbm, store.at[0]),
        pltpu.make_async_copy(tadj_ref, tadj_hbm, store.at[1]),
        pltpu.make_async_copy(sgrad_ref, sgrad_hbm, store.at[2]),
    ]
    stores[0].start()
    stores[1].start()

    for g in range(4):
        arrive(ag.at[0, pl.ds(max(4 * g, 1), 4 if g else 3)], 18 + g)
        for m in range(1, NX):
            post(ag.at[0, pl.ds(4 * g, 4)], ag.at[m, pl.ds(4 * g, 4)], 22, at(dx=m))
    arrive(t4.at[pl.ds(1, NTG - 1)], 6)
    for p in range(NTG):
        rows, lanes = slice(p // 2 * 8, p // 2 * 8 + 8), slice(p % 2 * 128, p % 2 * 128 + 128)
        sgrad_ref[rows, lanes] = t4[(tgt - p + NTG) % NTG]
    stores[2].start()

    arrive(ag.at[pl.ds(1, 3)], 22)

    for c in range(COLS // 128):
        for h in range(2):
            o = 2 * c + h
            ox, oy, oz = o // NYZ, (o // NZ) % NY, o % NZ
            slot = ((y - oy + NY) % NY) * NZ + (z - oz + NZ) % NZ
            tgrad_ref[16 * h : 16 * h + 16, c * 128 : c * 128 + 128] = ag[(x - ox + NX) % NX, slot]
        if c % 8 == 7:
            lanes = pl.ds((c - 7) * 128, 1024)
            stores.append(pltpu.make_async_copy(tgrad_ref.at[:, lanes], tgrad_hbm.at[:, lanes], store.at[3 + c // 8]))
            stores[-1].start()

    def sent(ref, sem):
        pltpu.make_async_copy(ref, ref, send.at[sem]).wait()

    sent(t1r, 0)
    sent(a1r, 1)
    sent(a1q, 2)
    sent(qr, 3)
    sent(t2r, 4)
    sent(qq, 5)
    sent(t4.at[pl.ds(1, NTG - 1)], 6)
    for g in range(4):
        sent(rxc.at[g], 8 + g)
        sent(rxv.at[g], 12 + g)
        sent(ag.at[0, pl.ds(max(4 * g, 1), 4 if g else 3)], 18 + g)
    sent(ryc, 16)
    sent(ryv, 17)
    sent(ag.at[pl.ds(1, 3)], 22)
    for c in stores:
        c.wait()


def deliver(*refs):
    sources, targets, held, sem_in, sem_out = refs[:4], refs[4:8], refs[8:12], refs[12], refs[13]
    parts = [(i, slice(None)) for i in range(3)] + [(3, pl.ds(8 * k, 8)) for k in range(4)]
    fetch = [pltpu.make_async_copy(sources[i].at[r], held[i].at[r], sem_in.at[n]) for n, (i, r) in enumerate(parts)]
    store = [pltpu.make_async_copy(held[i].at[r], targets[i].at[r], sem_out.at[n]) for n, (i, r) in enumerate(parts)]
    for c in fetch:
        c.start()
    for a, b in zip(fetch, store):
        a.wait()
        b.start()
    for c in store:
        c.wait()


def solution(mesh):
    def local(xs, xpot, xcot, ys, ypot, ycot):
        count = xs.shape[1] * mesh.shape["src"] * ys.shape[1] * mesh.shape["tgt"]
        hbm = pl.BlockSpec(memory_space=pltpu.HBM)
        results = (
            jax.ShapeDtypeStruct((1, ROWS), F32),
            jax.ShapeDtypeStruct((1, COLS), F32),
            jax.ShapeDtypeStruct((D, ROWS), F32),
            jax.ShapeDtypeStruct((D, COLS), F32),
        )
        outs = pl.pallas_call(
            functools.partial(kernel, -0.5 * math.log2(count)),
            out_shape=results,
            in_specs=[hbm] * 6,
            out_specs=(hbm,) * 4,
            scratch_shapes=[
                pltpu.VMEM((D, ROWS), F32),
                pltpu.VMEM((1, ROWS), F32),
                pltpu.VMEM((1, ROWS), F32),
                pltpu.VMEM((D, COLS), F32),
                pltpu.VMEM((1, COLS), F32),
                pltpu.VMEM((1, COLS), F32),
                pltpu.VMEM((1, ROWS), F32),
                pltpu.VMEM((1, COLS), F32),
                pltpu.VMEM((D, ROWS), F32),
                pltpu.VMEM((D, COLS), F32),
                pltpu.VMEM((2, 224, CHUNK), BF16),
                pltpu.VMEM((ROWS, COLS), BF16),
                pltpu.VMEM((ROWS, COLS), BF16),
                pltpu.VMEM((1, COLS), F32),
                pltpu.VMEM((1, COLS), F32),
                pltpu.VMEM((64, COLS), F32),
                pltpu.VMEM((D, COLS), F32),
                pltpu.VMEM((D, COLS), F32),
                pltpu.VMEM((1, 2 * ROWS), F32),
                pltpu.VMEM((NTG - 1, 1, 2 * ROWS), F32),
                pltpu.VMEM((1, COLS), F32),
                pltpu.VMEM((NZ - 1, 1, COLS), F32),
                pltpu.VMEM((1, COLS), F32),
                pltpu.VMEM((NX * NY - 1, 1, COLS), F32),
                pltpu.VMEM((NX * NYZ, 16, 128), F32),
                pltpu.VMEM((NX * NYZ, 16, 128), F32),
                pltpu.VMEM((4, NX - 1, 4, 16, 128), F32),
                pltpu.VMEM((4, NX - 1, 4, 16, 128), F32),
                pltpu.VMEM((NYZ, 16, 128), F32),
                pltpu.VMEM((NYZ, 16, 128), F32),
                pltpu.VMEM((NYZ - 1, 16, 128), F32),
                pltpu.VMEM((NYZ - 1, 16, 128), F32),
                pltpu.VMEM((NTG, 2, 8, 128), F32),
                pltpu.VMEM((NTG - 1, 2, 8, 128), F32),
                pltpu.VMEM((NTG, 8, 128), F32),
                pltpu.VMEM((1, 512), F32),
                pltpu.VMEM((NX * NTG - 1, 1, 512), F32),
                pltpu.VMEM((1, 512), F32),
                pltpu.VMEM((NYZ - 1, 1, 512), F32),
                pltpu.VMEM((NX, NYZ, 16, 128), F32),
                pltpu.SemaphoreType.DMA((9,)),
                pltpu.SemaphoreType.DMA((7,)),
                pltpu.SemaphoreType.DMA((23,)),
                pltpu.SemaphoreType.DMA((23,)),
            ],
            compiler_params=pltpu.CompilerParams(
                collective_id=0, has_side_effects=True, vmem_limit_bytes=60 * 2**20
            ),
        )(xs, xpot.reshape(1, ROWS), xcot.reshape(1, ROWS), ys, ypot.reshape(1, COLS), ycot.reshape(1, COLS))
        sadj, tadj, sgrad, tgrad = pl.pallas_call(
            deliver,
            out_shape=results,
            in_specs=[hbm] * 4,
            out_specs=(hbm,) * 4,
            scratch_shapes=[pltpu.VMEM(r.shape, F32) for r in results]
            + [pltpu.SemaphoreType.DMA((7,)), pltpu.SemaphoreType.DMA((7,))],
            compiler_params=pltpu.CompilerParams(vmem_limit_bytes=60 * 2**20),
        )(*outs)
        return sadj.reshape(ROWS), tadj.reshape(COLS), sgrad, tgrad

    return jax.shard_map(
        local,
        mesh=mesh,
        in_specs=(P(None, "src"), P("src"), P("src"), P(None, "tgt"), P("tgt"), P("tgt")),
        out_specs=(P("src"), P("tgt"), P(None, "src"), P(None, "tgt")),
        check_vma=False,
    )
```

time: 72.9 us -> 60.5 us (0.83)
  the two profiles are of different devices: /device:TPU:1 before, /device:TPU:8 now
where the time goes in v2:
time: 60.5 us; the launch traced here: 60.4 us
  Pallas kernels  59.7 us (99%)
  between operations  0.64 us (1%)
    pallas_call x1, Pallas kernels, local(): pl.pallas_call(functools.partial(kernel, -0.5 * math.log2(count)), out_sh...  57.8 us
    pallas_call x1, Pallas kernels, local(): pl.pallas_call(deliver, out_shape=results, in_specs=[hbm] * 4, out_specs=...  1.91 us

profile of v2, /device:TPU:8, one launch (start us, length us, event | category | flops | bytes accessed | tf_op | source)
XLA Modules:
  0.0 60.4 jit_solution(7594176896847201233)
XLA Ops:
  0.6 57.8 %shard_map.93 = (f32[1,256]{1,0:T(1,128)}, f32[1,4096]{1,0:T(1,128)}, f32[32,256]{1,0:T(8,128)}, f32[32,4096]{1,0:T(8,128)}) custom-call(f32[32,256]{1,0:T(8,128)} %xs_hbm.1, f32[1,256]{1,0:T(1,128)} %bitcast.8, f32[1,256]{1,0:T(1,128)} %bitcast.9, f32[32,4096]{1,0:T(8,128)} %ys_hbm.1, f32[1,4096]{1,0:T(1,128)} %bitcast.6, f32[1,4096]{1,0:T(1,128)} %bitcast.7), custom_call_target="tpu_custom_call" | custom-call | tf_op jit(solution)/shard_map/pallas_call | solution.py:423
  58.5 1.9 %shard_map.94 = (f32[1,256]{1,0:T(1,128)}, f32[1,4096]{1,0:T(1,128)}, f32[32,256]{1,0:T(8,128)}, f32[32,4096]{1,0:T(8,128)}) custom-call(f32[1,256]{1,0:T(1,128)} %get-tuple-element.12.refs_0_, f32[1,4096]{1,0:T(1,128)} %get-tuple-element.13.refs_1_, f32[32,256]{1,0:T(8,128)} %get-tuple-element.14.refs_2_, f32[32,4096]{1,0:T(8,128)} %get-tuple-element.15.refs_3_), custom_call_target="tpu_custom_call" | custom-call | tf_op jit(solution)/shard_map/pallas_call | solution.py:478

commit v3 on v2

--- a/solution.py
+++ b/solution.py
@@ -20,7 +20,6 @@
 COLS = 4096
 CHUNK = 512
 RIDGE = 0.5
-LOG2E = 1.4426950408889634
 
 
 def split2(v):
@@ -48,7 +47,7 @@
 
 
 def kernel(
-    factor_log2,
+    factor_log,
     xs_hbm, xpot_hbm, xcot_hbm, ys_hbm, ypot_hbm, ycot_hbm,
     sadj_hbm, tadj_hbm, sgrad_hbm, tgrad_hbm,
     xs_ref, xpot_ref, xcot_ref, ys_ref, ypot_ref, ycot_ref,
@@ -56,7 +55,7 @@
     bk, ph, pl_, cm_ref, pcs_ref, work, ubuf, wbuf,
     t1s, t1r, a1s, a1r, a1m, a1q,
     gc, gv, rxc, rxv, hc, hv, ryc, ryv,
-    t2s, t2r, t4, qs, qr, qm, qq, ag,
+    t2s, t2r, t4, qs, qr, qm, qq, qn, qz, ag,
     load, store, send, recv,
 ):
     loads = [
@@ -88,15 +87,14 @@
     def arrive(ref, sem):
         pltpu.make_async_copy(ref, ref, recv.at[sem]).wait()
 
-    z_peers = [dict(dz=k) for k in range(1, NZ)]
-    xy_peers = [dict(dx=k // NY, dy=k % NY) for k in range(1, NX * NY)]
+    z_peers = [dict(dz=k) for k in (4, 3, 5, 2, 6, 1, 7)]
+    xy_peers = [dict(dx=k // NY, dy=k % NY) for k in (5, 3, 7, 1, 4, 2, 6)]
     yz_peers = [dict(dy=k // NZ, dz=k % NZ) for k in range(1, NYZ)]
     x_peers = [dict(dx=k) for k in range(1, NX)]
-    t_peers = [dict(dt=k) for k in range(1, NTG)]
-    tx_peers = [dict(dx=k // NTG, dt=k % NTG) for k in range(1, NX * NTG)]
+    t_peers = [dict(dt=k) for k in (4, 3, 5, 2, 6, 1, 7)]
 
     barrier = pltpu.get_barrier_semaphore()
-    greet = tx_peers + yz_peers + [p for p in xy_peers if p["dx"] and p["dy"]]
+    greet = yz_peers + [p for p in xy_peers if p["dx"]] + t_peers
     for p in greet:
         pl.semaphore_signal(barrier, inc=1, device_id=at(**p), device_id_type=MESH)
 
@@ -105,8 +103,8 @@
     xs = xs_ref[...]
     cs = xcot_ref[...]
     ct = ycot_ref[...]
-    x1, x2, x3 = split3(xs * (4.0 * LOG2E))
-    row_term = (xpot_ref[...] - 2.0 * jnp.sum(xs * xs, axis=0, keepdims=True)) * LOG2E
+    x1, x2, x3 = split3(xs * 4.0)
+    row_term = (xpot_ref[...] - 2.0 * jnp.sum(xs * xs, axis=0, keepdims=True))
     r1, r2, r3 = split3(row_term)
     one_r = jnp.ones((1, ROWS), F32)
     tail_a = jnp.concatenate(
@@ -130,14 +128,14 @@
         yc = ys_ref[:, at_c]
         ctc = ycot_ref[:, at_c]
         y1, y2, y3 = split3(yc)
-        col_term = (ypot_ref[:, at_c] - 2.0 * jnp.sum(yc * yc, axis=0, keepdims=True)) * LOG2E
-        c1, c2, c3 = split3(col_term + factor_log2)
+        col_term = (ypot_ref[:, at_c] - 2.0 * jnp.sum(yc * yc, axis=0, keepdims=True))
+        c1, c2, c3 = split3(col_term + factor_log)
         tail_b = jnp.concatenate(
             [one_c, one_c, one_c, c1.astype(F32), c2.astype(F32), c3.astype(F32),
              jnp.zeros((26, CHUNK), F32)], axis=0,
         ).astype(BF16)
         bk[i % 2] = jnp.concatenate([y1, y2, y1, y2, y3, y1, tail_b], axis=0)
-        plan = jnp.exp2(dot_tn(ak, bk[i % 2]))
+        plan = jnp.exp(dot_tn(ak, bk[i % 2]))
         high, low = split2(plan)
         ph[:, at_c] = high
         pl_[:, at_c] = low
@@ -159,10 +157,10 @@
 
     pl.semaphore_wait(barrier, len(greet))
 
+    for i, p in enumerate(z_peers):
+        post(a1s, a1r.at[i], 1, at(**p))
     for i, p in enumerate(t_peers):
         post(t1s, t1r.at[i], 0, at(**p))
-    for i, p in enumerate(z_peers):
-        post(a1s, a1r.at[i], 1, at(**p))
 
     def col_products(vectors, width):
         high, low = split2(vectors)
@@ -202,7 +200,7 @@
 
     def post_x(buf, into, base):
         for g in (3, 2, 1, 0):
-            for m in range(1, NX):
+            for m in (2, 1, 3):
                 post(buf.at[pl.ds(m * NYZ + 4 * g, 4)], into.at[g, m - 1], base + g, at(dx=m))
 
     post_x(gc, rxc, 8)
@@ -218,6 +216,13 @@
         lanes = slice(c * 128, c * 128 + 128)
         wbuf[:, lanes] = work[32:33, lanes] * ys_ref[:, lanes] - work[0:32, lanes]
 
+
+    def fold(v):
+        acc = v[:, 0:128]
+        for c in range(1, v.shape[1] // 128):
+            acc = acc + v[:, c * 128 : c * 128 + 128]
+        return acc
+
     arrive(a1r, 1)
     total = a1s[...]
     for i in range(NZ - 1):
@@ -225,6 +230,7 @@
     a1m[...] = total
     for i, p in enumerate(xy_peers):
         post(a1m, a1q.at[i], 2, at(**p))
+
 
     def make_c(at_c):
         yc = ys_ref[:, at_c]
@@ -257,26 +263,19 @@
     post_x(gv, rxv, 12)
     tadj_ref[...] = vt
 
-    def fold(v):
-        acc = v[:, 0:128]
-        for c in range(1, v.shape[1] // 128):
-            acc = acc + v[:, c * 128 : c * 128 + 128]
-        return acc
-
     of_src, of_tgt = 1.0 / NTG, 1.0 / (NX * NYZ)
     ct = ycot_ref[...]
-    pvs_part = work[32:33, :]
     qs[...] = jnp.concatenate(
         [
             fold(cs * cs) * of_src + fold(ct * ct) * of_tgt,
             fold(cs * vs) * of_src + fold(ct * vt) * of_tgt,
             fold(vs * vs) * of_src + fold(vt * vt) * of_tgt,
-            fold(rm_part * vs * vs) + fold(vt * (cm_ref[...] * vt + 2.0 * pvs_part)),
+            fold(rm_part * vs * vs) + fold(vt * (cm_ref[...] * vt + 2.0 * work[32:33, :])),
         ],
         axis=1,
     )
-    for i, p in enumerate(tx_peers):
-        post(qs, qr.at[i], 3, at(**p))
+    for i, p in enumerate(t_peers):
+        post(qs, qr.at[i], 7, at(**p))
 
     def make_v(at_c):
         v = tadj_ref[:, at_c]
@@ -290,17 +289,25 @@
         t2s[slot, 0] = row_c[rows, lanes]
         t2s[slot, 1] = row_v[rows, lanes]
     for i, p in enumerate(t_peers):
-        post(t2s.at[i + 1], t2r.at[i], 4, at(**p))
-
-    add_x(gv, rxv, hv, ryv, 12, 17)
-
-    arrive(qr, 3)
+        post(t2s.at[p["dt"]], t2r.at[i], 4, at(**p))
+
+    arrive(qr, 7)
     inner = qs[...]
-    for i in range(NX * NTG - 1):
+    for i in range(NTG - 1):
         inner = inner + qr[i]
     qm[...] = inner
-    for i, p in enumerate(yz_peers):
-        post(qm, qq.at[i], 5, at(**p))
+    for i, p in enumerate(xy_peers):
+        post(qm, qq.at[i], 23, at(**p))
+
+    add_x(gv, rxv, hv, ryv, 12, 17)
+
+    arrive(qq, 23)
+    inner = qm[...]
+    for i in range(NX * NY - 1):
+        inner = inner + qq[i]
+    qn[...] = inner
+    for i, p in enumerate(z_peers):
+        post(qn, qz.at[i], 3, at(**p))
 
     arrive(ryc, 16)
     piece_c = hc[0]
@@ -311,10 +318,10 @@
     for i in range(NTG - 1):
         row_piece = row_piece + t2r[i]
 
-    arrive(qq, 5)
-    inner = qm[...]
-    for i in range(NYZ - 1):
-        inner = inner + qq[i]
+    arrive(qz, 3)
+    inner = qn[...]
+    for i in range(NZ - 1):
+        inner = inner + qz[i]
     m0, g1, g2, g3 = (
         jnp.sum(inner[:, q * 128 : q * 128 + 128], axis=1, keepdims=True) for q in range(4)
     )
@@ -336,12 +343,12 @@
     for s in range(NYZ - 1):
         piece_v = piece_v + ryv[s]
     ag[0, 0] = k_c * piece_c + k_v * piece_v
-    for s in range(NYZ - 1, 0, -1):
+    for s in (12, 11, 13, 10, 14, 9, 15, 8, 4, 3, 5, 2, 6, 1, 7):
         post(ag.at[0, 0], ag.at[0, s], 18 + s // 4, at(dy=s // NZ, dz=s % NZ))
 
     t4[0] = k_c * row_piece[0] + k_v * row_piece[1]
     for i, p in enumerate(t_peers):
-        post(t4.at[0], t4.at[i + 1], 6, at(**p))
+        post(t4.at[0], t4.at[p["dt"]], 6, at(**p))
     sadj_ref[...] = of_c * cs + of_v * vs
     tadj_ref[...] = of_c * ct + of_v * vt
     stores = [
@@ -354,7 +361,7 @@
 
     for g in range(4):
         arrive(ag.at[0, pl.ds(max(4 * g, 1), 4 if g else 3)], 18 + g)
-        for m in range(1, NX):
+        for m in (2, 1, 3):
             post(ag.at[0, pl.ds(4 * g, 4)], ag.at[m, pl.ds(4 * g, 4)], 22, at(dx=m))
     arrive(t4.at[pl.ds(1, NTG - 1)], 6)
     for p in range(NTG):
@@ -381,9 +388,10 @@
     sent(t1r, 0)
     sent(a1r, 1)
     sent(a1q, 2)
-    sent(qr, 3)
+    sent(qz, 3)
     sent(t2r, 4)
-    sent(qq, 5)
+    sent(qr, 7)
+    sent(qq, 23)
     sent(t4.at[pl.ds(1, NTG - 1)], 6)
     for g in range(4):
         sent(rxc.at[g], 8 + g)
@@ -421,7 +429,7 @@
             jax.ShapeDtypeStruct((D, COLS), F32),
         )
         outs = pl.pallas_call(
-            functools.partial(kernel, -0.5 * math.log2(count)),
+            functools.partial(kernel, -0.5 * math.log(count)),
             out_shape=results,
             in_specs=[hbm] * 6,
             out_specs=(hbm,) * 4,
@@ -462,14 +470,16 @@
                 pltpu.VMEM((NTG - 1, 2, 8, 128), F32),
                 pltpu.VMEM((NTG, 8, 128), F32),
                 pltpu.VMEM((1, 512), F32),
-                pltpu.VMEM((NX * NTG - 1, 1, 512), F32),
+                pltpu.VMEM((NTG - 1, 1, 512), F32),
                 pltpu.VMEM((1, 512), F32),
-                pltpu.VMEM((NYZ - 1, 1, 512), F32),
+                pltpu.VMEM((NX * NY - 1, 1, 512), F32),
+                pltpu.VMEM((1, 512), F32),
+                pltpu.VMEM((NZ - 1, 1, 512), F32),
                 pltpu.VMEM((NX, NYZ, 16, 128), F32),
                 pltpu.SemaphoreType.DMA((9,)),
                 pltpu.SemaphoreType.DMA((7,)),
-                pltpu.SemaphoreType.DMA((23,)),
-                pltpu.SemaphoreType.DMA((23,)),
+                pltpu.SemaphoreType.DMA((24,)),
+                pltpu.SemaphoreType.DMA((24,)),
             ],
             compiler_params=pltpu.CompilerParams(
                 collective_id=0, has_side_effects=True, vmem_limit_bytes=60 * 2**20

time: 60.5 us -> 57.6 us (0.952)
  the two profiles are of different devices: /device:TPU:8 before, /device:TPU:16 now
where the time goes in v3:
time: 57.6 us; the launch traced here: 57.4 us
  Pallas kernels  56.8 us (99%)
  between operations  0.64 us (1%)
    pallas_call x1, Pallas kernels, local(): pl.pallas_call(functools.partial(kernel, -0.5 * math.log(count)), out_sha...  54.9 us
    pallas_call x1, Pallas kernels, local(): pl.pallas_call(deliver, out_shape=results, in_specs=[hbm] * 4, out_specs=...  1.91 us

profile of v3, /device:TPU:16, one launch (start us, length us, event | category | flops | bytes accessed | tf_op | source)
XLA Modules:
  0.0 57.4 jit_solution(1730015831017873300)
XLA Ops:
  0.6 54.9 %shard_map.93 = (f32[1,256]{1,0:T(1,128)}, f32[1,4096]{1,0:T(1,128)}, f32[32,256]{1,0:T(8,128)}, f32[32,4096]{1,0:T(8,128)}) custom-call(f32[32,256]{1,0:T(8,128)} %xs_hbm.1, f32[1,256]{1,0:T(1,128)} %bitcast.8, f32[1,256]{1,0:T(1,128)} %bitcast.9, f32[32,4096]{1,0:T(8,128)} %ys_hbm.1, f32[1,4096]{1,0:T(1,128)} %bitcast.6, f32[1,4096]{1,0:T(1,128)} %bitcast.7), custom_call_target="tpu_custom_call" | custom-call | tf_op jit(solution)/shard_map/pallas_call | solution.py:431
  55.5 1.9 %shard_map.94 = (f32[1,256]{1,0:T(1,128)}, f32[1,4096]{1,0:T(1,128)}, f32[32,256]{1,0:T(8,128)}, f32[32,4096]{1,0:T(8,128)}) custom-call(f32[1,256]{1,0:T(1,128)} %get-tuple-element.12.refs_0_, f32[1,4096]{1,0:T(1,128)} %get-tuple-element.13.refs_1_, f32[32,256]{1,0:T(8,128)} %get-tuple-element.14.refs_2_, f32[32,4096]{1,0:T(8,128)} %get-tuple-element.15.refs_3_), custom_call_target="tpu_custom_call" | custom-call | tf_op jit(solution)/shard_map/pallas_call | solution.py:488

commit v4 on v3

--- a/solution.py
+++ b/solution.py
@@ -18,6 +18,7 @@
 D = 32
 ROWS = 256
 COLS = 4096
+XCOLS = COLS // NX
 CHUNK = 512
 RIDGE = 0.5
 
@@ -362,25 +363,27 @@
     for g in range(4):
         arrive(ag.at[0, pl.ds(max(4 * g, 1), 4 if g else 3)], 18 + g)
         for m in (2, 1, 3):
-            post(ag.at[0, pl.ds(4 * g, 4)], ag.at[m, pl.ds(4 * g, 4)], 22, at(dx=m))
+            post(ag.at[0, pl.ds(4 * g, 4)], ag.at[m, pl.ds(4 * g, 4)], 23 + m, at(dx=m))
     arrive(t4.at[pl.ds(1, NTG - 1)], 6)
     for p in range(NTG):
         rows, lanes = slice(p // 2 * 8, p // 2 * 8 + 8), slice(p % 2 * 128, p % 2 * 128 + 128)
         sgrad_ref[rows, lanes] = t4[(tgt - p + NTG) % NTG]
     stores[2].start()
 
-    arrive(ag.at[pl.ds(1, 3)], 22)
-
-    for c in range(COLS // 128):
-        for h in range(2):
-            o = 2 * c + h
-            ox, oy, oz = o // NYZ, (o // NZ) % NY, o % NZ
-            slot = ((y - oy + NY) % NY) * NZ + (z - oz + NZ) % NZ
-            tgrad_ref[16 * h : 16 * h + 16, c * 128 : c * 128 + 128] = ag[(x - ox + NX) % NX, slot]
-        if c % 8 == 7:
-            lanes = pl.ds((c - 7) * 128, 1024)
-            stores.append(pltpu.make_async_copy(tgrad_ref.at[:, lanes], tgrad_hbm.at[:, lanes], store.at[3 + c // 8]))
-            stores[-1].start()
+    def put(m):
+        ox = (x - m + NX) % NX
+        for k in range(NYZ):
+            slot = ((y - k // NZ + NY) % NY) * NZ + (z - k % NZ + NZ) % NZ
+            lanes = pl.ds(pl.multiple_of(ox * XCOLS + k // 2 * 128, 128), 128)
+            tgrad_ref[16 * (k % 2) : 16 * (k % 2) + 16, lanes] = ag[m, slot]
+        lanes = pl.ds(pl.multiple_of(ox * XCOLS, XCOLS), XCOLS)
+        stores.append(pltpu.make_async_copy(tgrad_ref.at[:, lanes], tgrad_hbm.at[:, lanes], store.at[3 + m]))
+        stores[-1].start()
+
+    put(0)
+    for m in (1, 3, 2):
+        arrive(ag.at[m], 23 + m)
+        put(m)
 
     def sent(ref, sem):
         pltpu.make_async_copy(ref, ref, send.at[sem]).wait()
@@ -399,7 +402,8 @@
         sent(ag.at[0, pl.ds(max(4 * g, 1), 4 if g else 3)], 18 + g)
     sent(ryc, 16)
     sent(ryv, 17)
-    sent(ag.at[pl.ds(1, 3)], 22)
+    for m in range(1, NX):
+        sent(ag.at[m], 23 + m)
     for c in stores:
         c.wait()
 
@@ -478,8 +482,8 @@
                 pltpu.VMEM((NX, NYZ, 16, 128), F32),
                 pltpu.SemaphoreType.DMA((9,)),
                 pltpu.SemaphoreType.DMA((7,)),
-                pltpu.SemaphoreType.DMA((24,)),
-                pltpu.SemaphoreType.DMA((24,)),
+                pltpu.SemaphoreType.DMA((27,)),
+                pltpu.SemaphoreType.DMA((27,)),
             ],
             compiler_params=pltpu.CompilerParams(
                 collective_id=0, has_side_effects=True, vmem_limit_bytes=60 * 2**20

time: 57.6 us -> 57.5 us (level)
  no operation moved by 1% of the time
where the time goes in v4:
time: 57.5 us; the launch traced here: 57.3 us
  Pallas kernels  56.7 us (99%)
  between operations  0.64 us (1%)
    pallas_call x1, Pallas kernels, local(): pl.pallas_call(functools.partial(kernel, -0.5 * math.log(count)), out_sha...  54.8 us
    pallas_call x1, Pallas kernels, local(): pl.pallas_call(deliver, out_shape=results, in_specs=[hbm] * 4, out_specs=...  1.91 us

profile of v4, /device:TPU:16, one launch (start us, length us, event | category | flops | bytes accessed | tf_op | source)
XLA Modules:
  0.0 57.3 jit_solution(14805047010115601745)
XLA Ops:
  0.6 54.8 %shard_map.93 = (f32[1,256]{1,0:T(1,128)}, f32[1,4096]{1,0:T(1,128)}, f32[32,256]{1,0:T(8,128)}, f32[32,4096]{1,0:T(8,128)}) custom-call(f32[32,256]{1,0:T(8,128)} %xs_hbm.1, f32[1,256]{1,0:T(1,128)} %bitcast.8, f32[1,256]{1,0:T(1,128)} %bitcast.9, f32[32,4096]{1,0:T(8,128)} %ys_hbm.1, f32[1,4096]{1,0:T(1,128)} %bitcast.6, f32[1,4096]{1,0:T(1,128)} %bitcast.7), custom_call_target="tpu_custom_call" | custom-call | tf_op jit(solution)/shard_map/pallas_call | solution.py:435
  55.4 1.9 %shard_map.94 = (f32[1,256]{1,0:T(1,128)}, f32[1,4096]{1,0:T(1,128)}, f32[32,256]{1,0:T(8,128)}, f32[32,4096]{1,0:T(8,128)}) custom-call(f32[1,256]{1,0:T(1,128)} %get-tuple-element.12.refs_0_, f32[1,4096]{1,0:T(1,128)} %get-tuple-element.13.refs_1_, f32[32,256]{1,0:T(8,128)} %get-tuple-element.14.refs_2_, f32[32,4096]{1,0:T(8,128)} %get-tuple-element.15.refs_3_), custom_call_target="tpu_custom_call" | custom-call | tf_op jit(solution)/shard_map/pallas_call | solution.py:492
